TPU v7x, 32 devices: a whole 2x2x4 slice. The times are simulated.
32 devices in a mesh: row: 4 (over x, core), col: 8 (over z, y).
Axes of the slice: x: 2, y: 2, z: 4, core: 2. Of those that a mesh axis runs over, the one named last changes fastest.
Arguments:
- kernel: float32 [2048, 2048], P('row', 'col'), may hold values from -6 to 6
- margin: float32 [2048, 2048], P('row', 'col'), may hold values from -0.0029296875 to 0.0029296875
- grid_values: bfloat16 [2048, 16384], P(None, 'col'), may hold values from -0.125 to 0.125
- proj_margins: bfloat16 [2048, 4096], P(None, 'col'), may hold values from -0.125 to 0.125
- kernel_pattern: int32 [16, 16], replicated, may hold values 0 or 1
- margin_pattern: int32 [16, 16], replicated, may hold values 0 or 1
- box_pattern: int32 [128, 16], P('col'), may hold values 0 or 1
- proj_pattern: int32 [256, 16], P('col'), may hold values 0 or 1
Outputs:
- kernel_out: float32 [2048, 2048], P('row', 'col')
- occupancy: float32 [256, 256], P('col')
- density: float32 [16384], P('col')
All inputs are finite; a program needn't handle non-finite values. No bound on the sum of `box_pattern` or of `proj_pattern` on one device may be relied on, other than what follows from the above.
Results may differ from a plain program's by a relative error of at most 0.0065.
Values may be sent and summed in bfloat16 or wider, within the bound.
A program may use at most 128 MiB of HBM per device.

v0:
```python
import functools

import jax
import jax.numpy as jnp
from jax import lax
from jax.experimental import pallas as pl
from jax.experimental.pallas import tpu as pltpu
from jax.sharding import PartitionSpec as P

TILE = 128
BOXPTS = 128
NPROJ = 16
PIECES = 2
SPAN = 512
F32 = jnp.float32
HALF = jnp.bfloat16
MESH = pl.DeviceIdType.MESH


def spot_at(place, n):
    if n == 8:
        turn = place // 4
        outer = place * (1 - turn) + (7 - place) * turn
        return outer * 2 + turn
    outer, inner = place // 4, place % 4
    odd = outer % 2
    return outer * 4 + inner * (1 - odd) + (3 - inner) * odd


def place_of(spot, n):
    if n == 8:
        outer, turn = spot // 2, spot % 2
        return outer * (1 - turn) + (7 - outer) * turn
    outer, inner = spot // 4, spot % 4
    odd = outer % 2
    return outer * 4 + inner * (1 - odd) + (3 - inner) * odd


def body(
    n_row,
    n_col,
    kernel_ref,
    margin_ref,
    grid_ref,
    proj_ref,
    kpat_ref,
    mpat_ref,
    box_ref,
    ppat_ref,
    out_ref,
    occ_ref,
    dens_ref,
    k_panel,
    m_panel,
    h_panel,
    s_col,
    k_col,
    w_col,
    points,
    mask,
    total,
    image,
    dens_acc,
    pay,
    ring_send,
    ring_recv,
    x_send,
    x_recv,
    core_send,
    core_recv,
    pay_send,
    pay_recv,
    load_sem,
):
    r = lax.axis_index("row")
    c = lax.axis_index("col")
    rows, cols = kernel_ref.shape
    n = rows * n_row
    gcols, pcols = grid_ref.shape[1], proj_ref.shape[1]
    nx = n_row // 2
    x, core = r // 2, r % 2
    place = place_of(c, n_col)

    def spot(k):
        return spot_at(lax.rem(place + k + n_col, n_col), n_col)

    ahead, behind = spot(1), spot(-1)
    others = [lax.rem(r + k, n_row) for k in range(1, n_row)]
    barrier = pltpu.get_barrier_semaphore()
    for other in others:
        pl.semaphore_signal(barrier, inc=1, device_id=(other, c), device_id_type=MESH)
    for other in (ahead, behind):
        pl.semaphore_signal(barrier, inc=1, device_id=(r, other), device_id_type=MESH)

    loads = [
        pltpu.make_async_copy(grid_ref, points.at[:, pl.ds(0, gcols)], load_sem.at[0]),
        pltpu.make_async_copy(proj_ref, points.at[:, pl.ds(gcols, pcols)], load_sem.at[1]),
    ]
    my_rows = pl.ds(pl.multiple_of(r * rows, rows), rows)
    for i in range(rows // TILE):
        for j in range(cols // TILE):
            a, b = pl.ds(i * TILE, TILE), pl.ds(j * TILE, TILE)
            keep = kpat_ref[r * (rows // TILE) + i, c * (cols // TILE) + j].astype(F32)
            block = (kernel_ref[a, b] * keep).astype(HALF)
            k_panel[c, a, b] = block
            k_col[pl.ds(pl.multiple_of(r * rows + i * TILE, TILE), TILE), b] = block
            keep = mpat_ref[r * (rows // TILE) + i, c * (cols // TILE) + j].astype(F32)
            s_col[pl.ds(pl.multiple_of(r * rows + i * TILE, TILE), TILE), b] = (
                margin_ref[a, b] * keep
            ).astype(HALF)

    pl.semaphore_wait(barrier, n_row + 1)
    sent = []

    part = rows // (2 * PIECES)

    def ring_copy(stage, panel, way, piece, step, origin):
        at = panel.at[origin, pl.ds((way * PIECES + piece) * part, part)]
        return pltpu.make_async_remote_copy(
            src_ref=at,
            dst_ref=at,
            send_sem=ring_send.at[stage, way, piece, step],
            recv_sem=ring_recv.at[stage, way, piece, step],
            device_id=(r, ahead if way == 0 else behind),
            device_id_type=MESH,
        )

    def origin_of(way, step):
        return spot(-step if way == 0 else step)

    def ring_start(stage, panel):
        for piece in range(PIECES):
            for way in range(2):
                copy = ring_copy(stage, panel, way, piece, 0, c)
                copy.start()
                sent.append(copy)

    def ring_step(stage, panel, step):
        for piece in range(PIECES):
            for way in range(2):
                origin = origin_of(way, step + 1)
                ring_copy(stage, panel, way, piece, step, origin).wait_recv()
                if step + 1 < n_col - 1:
                    copy = ring_copy(stage, panel, way, piece, step + 1, origin)
                    copy.start()
                    sent.append(copy)

    bit = rows // PIECES

    def x_copy(stage, panel, step, piece, origin):
        at = panel.at[pl.ds(pl.multiple_of(origin * rows + piece * bit, bit), bit)]
        return pltpu.make_async_remote_copy(
            src_ref=at,
            dst_ref=at,
            send_sem=x_send.at[stage, step, piece],
            recv_sem=x_recv.at[stage, step, piece],
            device_id=(lax.rem(x + 1, nx) * 2 + core, c),
            device_id_type=MESH,
        )

    def core_copy(stage, panel, step, piece, origin):
        at = panel.at[pl.ds(pl.multiple_of(origin * rows + piece * bit, bit), bit)]
        return pltpu.make_async_remote_copy(
            src_ref=at,
            dst_ref=at,
            send_sem=core_send.at[stage, step, piece],
            recv_sem=core_recv.at[stage, step, piece],
            device_id=(x * 2 + 1 - core, c),
            device_id_type=MESH,
        )

    def x_origin(step, side):
        return lax.rem(x - step + nx, nx) * 2 + side

    def row_start(stage, panel):
        for piece in range(PIECES):
            for make in (x_copy, core_copy):
                copy = make(stage, panel, 0, piece, r)
                copy.start()
                sent.append(copy)

    def row_relay(stage, panel, step):
        for piece in range(PIECES):
            origin = x_origin(step + 1, core)
            x_copy(stage, panel, step, piece, origin).wait_recv()
            onward = [core_copy(stage, panel, step + 1, piece, origin)]
            if step + 1 < nx - 1:
                onward.append(x_copy(stage, panel, step + 1, piece, origin))
            for copy in onward:
                copy.start()
                sent.append(copy)

    def row_wait(stage, panel, step):
        for piece in range(PIECES):
            core_copy(stage, panel, step, piece, x_origin(step, 1 - core)).wait_recv()

    def row_finish(stage, panel):
        for step in range(nx):
            row_wait(stage, panel, step)

    way_rows = rows // 2

    def multiply(panel, right, way, origin):
        half = pl.ds(way * way_rows, way_rows)
        deep = pl.ds(pl.multiple_of(origin * cols, cols), cols)
        total[half, :] += jnp.dot(
            panel[origin, half, :], right[deep, :], preferred_element_type=F32
        )

    def take(panel, right, step):
        for way in range(2):
            multiply(panel, right, way, origin_of(way, step))

    ring_start(0, k_panel)
    row_start(0, s_col)
    row_start(1, k_col)
    for load in loads:
        load.start()
    for ref, width, first in ((box_ref, BOXPTS, 0), (ppat_ref, NPROJ, gcols)):
        count = ref.shape[0]
        size = count * width
        spread = (
            lax.broadcasted_iota(jnp.int32, (count, size), 1) // width
            == lax.broadcasted_iota(jnp.int32, (count, size), 0)
        ).astype(F32)
        mask[:, pl.ds(first, size)] = lax.dot_general(
            ref[...].astype(F32), spread, (((0,), (0,)), ((), ())), preferred_element_type=F32
        )

    n_tiles = n // TILE

    def mask_tile(tile, _):
        at = pl.ds(pl.multiple_of(tile * TILE, TILE), TILE)
        keep = mask[pl.ds(tile, 1), :].astype(HALF)
        points[at, :] = points[at, :] * keep
        return 0

    total[...] = jnp.zeros_like(total)
    dens_acc[...] = jnp.zeros_like(dens_acc)
    image[...] = jnp.zeros_like(image)
    pay[...] = jnp.zeros_like(pay)
    for step in range(n_col - 1):
        ring_step(0, k_panel, step)
        if step == 2:
            for k in range(nx - 1):
                row_relay(0, s_col, k)
        if step == 4:
            row_finish(0, s_col)
            for k in range(step + 1):
                take(k_panel, s_col, k)
        if step > 4:
            take(k_panel, s_col, step)
        if step == 5:
            for k in range(nx - 1):
                row_relay(1, k_col, k)
    take(k_panel, s_col, n_col - 1)

    m_panel[c] = total[...].astype(HALF)
    ring_start(1, m_panel)
    row_finish(1, k_col)
    total[...] = jnp.zeros_like(total)
    take(m_panel, k_col, 0)
    for load in loads:
        load.wait()
    per = (n_tiles + n_col - 3) // (n_col - 2)
    for step in range(n_col - 1):
        ring_step(1, m_panel, step)
        take(m_panel, k_col, step + 1)
        if step < n_col - 2:
            lax.fori_loop(
                min(step * per, n_tiles), min((step + 1) * per, n_tiles), mask_tile, 0
            )

    w_col[my_rows, :] = total[...].astype(HALF)
    row_start(2, w_col)
    out_ref[...] = 3.0 * total[...]
    total[...] = jnp.zeros_like(total)
    span = rows // cols

    def quintic(origin):
        for k in range(span):
            for way in range(2):
                multiply(m_panel, w_col, way, origin * span + k)

    quintic(r)
    row_wait(2, w_col, 0)
    quintic(x * 2 + 1 - core)
    for step in range(nx - 1):
        row_relay(2, w_col, step)
        quintic(x_origin(step + 1, core))
        row_wait(2, w_col, step + 1)
        quintic(x_origin(step + 1, 1 - core))

    result = out_ref[...] - 2.0 * total[...]
    out_ref[...] = result
    h_panel[c] = result.astype(HALF)
    ring_start(2, h_panel)

    def apply(step):
        for way in range(2):
            origin = origin_of(way, step)
            half = pl.ds(way * way_rows, way_rows)
            deep = pl.ds(pl.multiple_of(origin * cols, cols), cols)
            local = pl.ds(pl.multiple_of(r * rows + way * way_rows, way_rows), way_rows)

            def tile(t, _):
                at = pl.ds(pl.multiple_of(t * SPAN, SPAN), SPAN)
                made = jnp.dot(
                    h_panel[origin, half, :], points[deep, at], preferred_element_type=F32
                )
                made = made * points[local, at].astype(F32)
                dens_acc[:, at] += jnp.sum(made.reshape(way_rows // 8, 8, SPAN), axis=0)
                return 0

            lax.fori_loop(0, gcols // SPAN, tile, 0)
            image[half, :] += jnp.dot(
                h_panel[origin, half, :],
                points[deep, pl.ds(gcols, pcols)],
                preferred_element_type=F32,
            )

    apply(0)
    for step in range(n_col - 1):
        ring_step(2, h_panel, step)
        apply(step + 1)

    for t in range(gcols // SPAN):
        pay[r, pl.ds(NPROJ + t, 1), :] = jnp.sum(
            dens_acc[:, pl.ds(t * SPAN, SPAN)], axis=0, keepdims=True
        )
    same = (
        lax.broadcasted_iota(jnp.int32, (TILE, TILE), 0) // NPROJ
        == lax.broadcasted_iota(jnp.int32, (TILE, TILE), 1) // NPROJ
    )
    for b in range(pcols // TILE):
        at = pl.ds(b * TILE, TILE)
        left = points[my_rows, pl.ds(gcols + b * TILE, TILE)]
        whole = image[:, at]
        high = whole.astype(HALF)
        low = (whole - high.astype(F32)).astype(HALF)
        dims = (((0,), (0,)), ((), ()))
        full = lax.dot_general(left, high, dims, preferred_element_type=F32)
        full += lax.dot_general(left, low, dims, preferred_element_type=F32)
        full = jnp.where(same, full, 0.0)
        pay[r, pl.ds(0, NPROJ), at] = jnp.sum(
            full.reshape(TILE // NPROJ, NPROJ, TILE), axis=0
        )

    def pay_copy(k, origin):
        return pltpu.make_async_remote_copy(
            src_ref=pay.at[origin],
            dst_ref=pay.at[origin],
            send_sem=pay_send.at[k],
            recv_sem=pay_recv.at[k],
            device_id=(others[k], c),
            device_id_type=MESH,
        )

    for k in range(n_row - 1):
        copy = pay_copy(k, r)
        copy.start()
        sent.append(copy)
    for k in range(n_row - 1):
        pay_copy(k, lax.rem(r - k - 1 + n_row, n_row)).wait_recv()
    gathered = pay[0]
    for k in range(1, n_row):
        gathered = gathered + pay[k]
    occ_ref[...] = gathered[:NPROJ]
    dens_ref[...] = gathered[NPROJ : NPROJ + gcols // SPAN]
    for copy in sent:
        copy.wait_send()


def on_device(
    n_row,
    n_col,
    kernel,
    margin,
    grid_values,
    proj_margins,
    kernel_pattern,
    margin_pattern,
    box_pattern,
    proj_pattern,
):
    rows, cols = kernel.shape
    n = rows * n_row
    gcols, pcols = grid_values.shape[1], proj_margins.shape[1]
    nx = n_row // 2
    dma = pltpu.SemaphoreType.DMA
    vmem = pl.BlockSpec(memory_space=pltpu.VMEM)
    smem = pl.BlockSpec(memory_space=pltpu.SMEM)
    far = pl.BlockSpec(memory_space=pl.ANY)
    out, occ, dens = pl.pallas_call(
        functools.partial(body, n_row, n_col),
        out_shape=(
            jax.ShapeDtypeStruct((rows, cols), F32),
            jax.ShapeDtypeStruct((NPROJ, pcols), F32),
            jax.ShapeDtypeStruct((gcols // SPAN, SPAN), F32),
        ),
        in_specs=[vmem, vmem, far, far, smem, smem, vmem, vmem],
        out_specs=(vmem, vmem, vmem),
        scratch_shapes=[
            pltpu.VMEM((n_col, rows, cols), HALF),
            pltpu.VMEM((n_col, rows, cols), HALF),
            pltpu.VMEM((n_col, rows, cols), HALF),
            pltpu.VMEM((n, cols), HALF),
            pltpu.VMEM((n, cols), HALF),
            pltpu.VMEM((n, cols), HALF),
            pltpu.VMEM((n, gcols + pcols), HALF),
            pltpu.VMEM((n // TILE, gcols + pcols), F32),
            pltpu.VMEM((rows, cols), F32),
            pltpu.VMEM((rows, pcols), F32),
            pltpu.VMEM((8, gcols), F32),
            pltpu.VMEM((n_row, NPROJ + 8, SPAN), F32),
            dma((3, 2, PIECES, n_col - 1)),
            dma((3, 2, PIECES, n_col - 1)),
            dma((3, nx - 1, PIECES)),
            dma((3, nx - 1, PIECES)),
            dma((3, nx, PIECES)),
            dma((3, nx, PIECES)),
            dma((n_row - 1,)),
            dma((n_row - 1,)),
            dma((2,)),
        ],
        compiler_params=pltpu.CompilerParams(
            collective_id=0, has_side_effects=True, vmem_limit_bytes=58 * 1024 * 1024
        ),
    )(
        kernel,
        margin,
        grid_values,
        proj_margins,
        kernel_pattern,
        margin_pattern,
        box_pattern,
        proj_pattern,
    )
    atoms = pcols // NPROJ
    occupancy = occ.reshape(NPROJ, atoms, NPROJ).transpose(1, 0, 2).reshape(atoms, NPROJ * NPROJ)
    return (out, occupancy, dens.reshape(gcols))


def solution(mesh):
    in_specs = (
        P("row", "col"),
        P("row", "col"),
        P(None, "col"),
        P(None, "col"),
        P(),
        P(),
        P("col", None),
        P("col", None),
    )
    out_specs = (P("row", "col"), P("col", None), P("col"))
    return jax.shard_map(
        functools.partial(on_device, mesh.shape["row"], mesh.shape["col"]),
        mesh=mesh,
        in_specs=in_specs,
        out_specs=out_specs,
        check_vma=False,
    )
```

profile of v0, /device:TPU:0, one launch (start us, length us, event | category | flops | bytes accessed | tf_op | source)
XLA Modules:
  0.0 108.5 jit_solution(13465583168416537392)
XLA Ops:
  0.6 1.4 %copy.13.ppat_ref = s32[32,16]{1,0:T(8,128)} copy(s32[32,16]{0,1:T(8,128)} %param.15) | data formatting | bytes 4096 | tf_op args[7]
  2.0 101.6 %shard_map.103 = (f32[512,256]{1,0:T(8,128)}, f32[16,512]{1,0:T(8,128)}, f32[4,512]{1,0:T(4,128)}) custom-call(f32[512,256]{1,0:T(8,128)} %kernel_ref.1, f32[512,256]{1,0:T(8,128)} %margin_ref.1, bf16[2048,2048]{1,0:T(8,128)(2,1)} %grid_ref.1, bf16[2048,512]{1,0:T(8,128)(2,1)} %proj_ref.1, s32[16,16]{1,0:T(8,128)} %kpat_ref.1, s32[16,16]{1,0:T(8,128)} %mpat_ref.1, ...), custom_call_target="tpu_custom_call" | custom-call | tf_op jit(solution)/shard_map/pallas_call | solution.py:394
  103.6 1.3 %copy.16 = f32[1,4,4,128]{3,1,2,0:T(4,128)} copy(f32[1,4,4,128]{3,2,1,0:T(4,128)} %bitcast.7) | data formatting | bytes 16384
  104.9 0.9 reshape.15
  105.8 0.1 copy.14
  105.9 0.7 copy.15
  106.6 1.9 %copy.18 = f32[512,256]{1,0:T(8,128)} copy(f32[512,256]{1,0:T(8,128)} %get-tuple-element.15) | data formatting | bytes 1048576
where the time goes:
time: 109 us
  Pallas kernels  102 us (94%)
  local copies, waits for them, and re-layouts  6.24 us (6%)
    pallas_call x1, Pallas kernels, on_device(): pl.pallas_call(functools.partial(body, n_row, n_col), out_shape=(jax.Shap...  102 us
    unnamed x4, local copies, waits for them, and re-layouts  5.24 us

commit v1 on v0

--- a/solution.py
+++ b/solution.py
@@ -10,7 +10,7 @@
 TILE = 128
 BOXPTS = 128
 NPROJ = 16
-PIECES = 2
+PIECES = 4
 SPAN = 512
 F32 = jnp.float32
 HALF = jnp.bfloat16
@@ -216,15 +216,15 @@
     row_start(1, k_col)
     for load in loads:
         load.start()
-    for ref, width, first in ((box_ref, BOXPTS, 0), (ppat_ref, NPROJ, gcols)):
-        count = ref.shape[0]
+    for ref, width, first, axis in ((box_ref, BOXPTS, 0, 0), (ppat_ref, NPROJ, gcols, 1)):
+        count = ref.shape[axis]
         size = count * width
         spread = (
             lax.broadcasted_iota(jnp.int32, (count, size), 1) // width
             == lax.broadcasted_iota(jnp.int32, (count, size), 0)
         ).astype(F32)
         mask[:, pl.ds(first, size)] = lax.dot_general(
-            ref[...].astype(F32), spread, (((0,), (0,)), ((), ())), preferred_element_type=F32
+            ref[...].astype(F32), spread, (((axis,), (0,)), ((), ())), preferred_element_type=F32
         )
 
     n_tiles = n // TILE
@@ -434,7 +434,7 @@
         kernel_pattern,
         margin_pattern,
         box_pattern,
-        proj_pattern,
+        proj_pattern.T,
     )
     atoms = pcols // NPROJ
     occupancy = occ.reshape(NPROJ, atoms, NPROJ).transpose(1, 0, 2).reshape(atoms, NPROJ * NPROJ)

time: 109 us -> 103 us (0.945)
  Pallas kernels: 102 us -> 96.9 us
  local copies, waits for them, and re-layouts: 6.24 us -> 4.86 us
    pallas_call x1, Pallas kernels: 102 us -> 96.9 us  [on_device(): pl.pallas_call(functools.partial(body, n_row, n_col), out_shape=(jax.Shap...]
    unnamed x4 -> x3, local copies, waits for them, and re-layouts: 5.24 us -> 3.87 us
where the time goes in v1:
time: 103 us; the launch traced here: 102 us
  Pallas kernels  96.9 us (94%)
  local copies, waits for them, and re-layouts  4.86 us (5%)
    pallas_call x1, Pallas kernels, on_device(): pl.pallas_call(functools.partial(body, n_row, n_col), out_shape=(jax.Shap...  96.9 us
    unnamed x3, local copies, waits for them, and re-layouts  3.87 us

profile of v1, /device:TPU:0, one launch (start us, length us, event | category | flops | bytes accessed | tf_op | source)
XLA Modules:
  0.0 102.4 jit_solution(13028787590834803051)
XLA Ops:
  0.6 96.9 %shard_map.103 = (f32[512,256]{1,0:T(8,128)}, f32[16,512]{1,0:T(8,128)}, f32[4,512]{1,0:T(4,128)}) custom-call(f32[512,256]{1,0:T(8,128)} %kernel_ref.1, f32[512,256]{1,0:T(8,128)} %margin_ref.1, bf16[2048,2048]{1,0:T(8,128)(2,1)} %grid_ref.1, bf16[2048,512]{1,0:T(8,128)(2,1)} %proj_ref.1, s32[16,16]{1,0:T(8,128)} %kpat_ref.1, s32[16,16]{1,0:T(8,128)} %mpat_ref.1, ...), custom_call_target="tpu_custom_call" | custom-call | tf_op jit(solution)/shard_map/pallas_call | solution.py:394
  97.6 1.3 %copy.14 = f32[1,4,4,128]{3,1,2,0:T(4,128)} copy(f32[1,4,4,128]{3,2,1,0:T(4,128)} %bitcast.8) | data formatting | bytes 16384
  98.9 0.9 reshape.15
  99.7 0.1 copy.12
  99.9 0.7 copy.13
  100.6 1.9 %copy.16 = f32[512,256]{1,0:T(8,128)} copy(f32[512,256]{1,0:T(8,128)} %get-tuple-element.15) | data formatting | bytes 1048576
